TPU v7x, 128 devices: a whole 4x4x4 slice. The times are simulated.
128 devices in a mesh: lat: 32 (over z, y, core), wave: 4 (over x).
Axes of the slice: x: 4, y: 4, z: 4, core: 2. Of those that a mesh axis runs over, the one named last changes fastest.
Arguments:
- spectra: float32 [1280, 2, 128, 640], P(('lat', 'wave')), may hold values from -0.01171875 to 0.01171875
- legendre: float32 [128, 1280, 2, 640], P(None, ('lat', 'wave')), may hold values from -4 to 4
- weights: float32 [128], replicated, may hold values from 1 to 4
- counts: int32 [128], P('lat'), may hold values from 5116 to 5632, as said below
- assign: int32 [1280], replicated, may hold values from 0 to 1279, as said below
Outputs:
- harmonic_products: float32 [1280, 2, 128, 640], P(('lat', 'wave'))
Inputs may be any that keep to these rules, and one draw needn't show every extreme that they name: `counts`: pair j has 5632 - 4 (127 - j) - 4 r points with r one of 0, 1, 2; the pair nearest the equator, j = 127, has exactly 5632. `assign`: A permutation of 0 to 1279 in which slots 2 s and 2 s + 1 hold a wavenumber m and 1279 - m.
All inputs are finite; a program needn't handle non-finite values.
Results may differ from a plain program's by a relative error of at most 0.0003.
Values sent between devices are 32-bit elements; how exact they have to be, the bound alone decides.
A program may use at most 128 MiB of HBM per device.

v0:
```python
import math

import jax
import jax.numpy as jnp
from jax import lax
from jax.sharding import PartitionSpec as P

PAD = 5632


HIGHEST_PRECISION = lax.Precision.HIGHEST


def block_rows(local_rows):
    for divisor in range(min(local_rows, 1536), 0, -1):
        if local_rows % divisor == 0:
            return divisor
    return 1


def inner_rows(block):
    for divisor in range(min(block, 128), 0, -1):
        if block % divisor == 0:
            return divisor
    return 1


def degree_mask(numbers, wave_total, half_degrees):
    degree = (
        2 * lax.iota(jnp.int32, half_degrees)[None, None, :] + lax.iota(jnp.int32, 2)[None, :, None]
    )
    return (degree < (wave_total - numbers)[:, None, None])[:, :, None, :]


def quadratic(physical_space_samples, atmosphere_layers):
    relative_rotation = physical_space_samples[:, :atmosphere_layers]
    velocity_spread = physical_space_samples[:, atmosphere_layers : 2 * atmosphere_layers]
    thermal_state = physical_space_samples[:, 2 * atmosphere_layers : 3 * atmosphere_layers]
    specific_humidity = physical_space_samples[:, 3 * atmosphere_layers :]
    return jnp.concatenate(
        [
            relative_rotation * thermal_state,
            velocity_spread * thermal_state,
            thermal_state * specific_humidity,
            specific_humidity * velocity_spread,
        ],
        axis=1,
    )


def pair_cycle(pair_lines, point_count, numbers, first_point, local_rows):
    line_total = pair_lines.shape[0]
    wave_total = pair_lines.shape[1]
    columns = pair_lines.shape[2] // 2
    doubled = jnp.where(numbers == 0, 1.0, 2.0).astype(jnp.float32)[:, None]

    def hemisphere_operand(line):
        return jnp.concatenate([line[:, :columns] * doubled, -line[:, columns:] * doubled], axis=0)

    weighted = jnp.concatenate(
        [hemisphere_operand(pair_lines[line_place]) for line_place in range(line_total)], axis=1
    )
    step_angle = 2.0 * math.pi / point_count.astype(jnp.float32)
    atmosphere_layers = columns // 4
    block = block_rows(local_rows)
    small_rows = inner_rows(block)
    group_total = block // small_rows
    inner_points = lax.iota(jnp.int32, small_rows)
    inner_angles = (inner_points[:, None] * numbers[None, :] % point_count).astype(
        jnp.float32
    ) * step_angle
    inner_cosine = jnp.cos(inner_angles)
    inner_sine = jnp.sin(inner_angles)

    def add_block(summed, leading_row):
        base_points = first_point + leading_row + lax.iota(jnp.int32, group_total) * small_rows
        base_angles = (base_points[:, None] * numbers[None, :] % point_count).astype(
            jnp.float32
        ) * step_angle
        base_cosine = jnp.cos(base_angles)[:, None, :]
        base_sine = jnp.sin(base_angles)[:, None, :]
        cosine_rows = (base_cosine * inner_cosine[None] - base_sine * inner_sine[None]).reshape(
            block, wave_total
        )
        sine_rows = (base_sine * inner_cosine[None] + base_cosine * inner_sine[None]).reshape(
            block, wave_total
        )
        basis_rows = jnp.concatenate([cosine_rows, sine_rows], axis=1)
        points = first_point + leading_row + lax.iota(jnp.int32, block)
        physical_space_samples = jnp.dot(
            basis_rows, weighted, precision=HIGHEST_PRECISION, preferred_element_type=jnp.float32
        )
        line_terms = jnp.concatenate(
            [
                quadratic(
                    physical_space_samples[:, line_place * columns : (line_place + 1) * columns],
                    atmosphere_layers,
                )
                for line_place in range(line_total)
            ],
            axis=1,
        )
        terms = jnp.where((points < point_count)[:, None], line_terms, 0.0)
        summed = summed + lax.dot_general(
            basis_rows,
            terms,
            (((0,), (0,)), ((), ())),
            precision=HIGHEST_PRECISION,
            preferred_element_type=jnp.float32,
        )
        return (summed, None)

    starts = lax.iota(jnp.int32, local_rows // block) * block
    summed, unused = lax.scan(
        add_block, jnp.zeros((2 * wave_total, line_total * columns), jnp.float32), starts
    )
    inverse = 1.0 / point_count.astype(jnp.float32)
    outputs = []
    for line_place in range(line_total):
        section = summed[:, line_place * columns : (line_place + 1) * columns]
        outputs.append(
            jnp.concatenate(
                [section[:wave_total] * inverse, -section[wave_total:] * inverse], axis=1
            )
        )
    return jnp.stack(outputs, axis=0)


def grid_work(latitude_lines, counts, numbers):
    wave_count = lax.axis_size("wave")
    local_rows = PAD // wave_count
    first_point = lax.axis_index("wave") * local_rows
    group_lines = lax.all_gather(latitude_lines, "wave", axis=0, tiled=True)

    def per_pair(couple_operand):
        pair_lines, point_count = couple_operand
        return pair_cycle(pair_lines, point_count, numbers, first_point, local_rows)

    partial_sums = lax.map(per_pair, (group_lines, counts))
    return lax.psum_scatter(partial_sums, "wave", scatter_dimension=0, tiled=True)


def body(spectra, legendre, weights, counts, assign):
    slot_count = spectra.shape[0]
    half_degrees = spectra.shape[3]
    wave_total = assign.shape[0]
    device_place = lax.axis_index(("lat", "wave"))
    own_numbers = lax.dynamic_slice_in_dim(assign, device_place * slot_count, slot_count)
    valid_degrees = degree_mask(own_numbers, wave_total, half_degrees)
    masked = jnp.where(valid_degrees, spectra, 0.0)
    parity = jnp.einsum("jspq,sprq->jpsr", legendre, masked, precision=HIGHEST_PRECISION)
    fourier = jnp.stack([parity[:, 0] + parity[:, 1], parity[:, 0] - parity[:, 1]], axis=1)
    returned = lax.all_to_all(
        grid_work(
            lax.all_to_all(fourier, ("lat", "wave"), split_axis=0, concat_axis=2, tiled=True),
            counts,
            assign,
        ),
        ("lat", "wave"),
        split_axis=2,
        concat_axis=0,
        tiled=True,
    )
    folded = weights[:, None, None, None] * jnp.stack(
        [returned[:, 0] + returned[:, 1], returned[:, 0] - returned[:, 1]], axis=1
    )
    result = jnp.einsum("jspq,jpsr->sprq", legendre, folded, precision=HIGHEST_PRECISION)
    return jnp.where(valid_degrees, result, 0.0)


def solution(mesh):
    placed = (
        P(("lat", "wave"), None, None, None),
        P(None, ("lat", "wave"), None, None),
        P(),
        P("lat"),
        P(),
    )
    return jax.shard_map(
        body,
        mesh=mesh,
        in_specs=placed,
        out_specs=P(("lat", "wave"), None, None, None),
        check_vma=False,
    )
```

profile of v0, /device:TPU:1, one launch (start us, length us, event | category | flops | bytes accessed | tf_op | source)
XLA Modules:
  0.0 485.2 jit_solution(12768286848308852770)
XLA Ops:
  7.4 11.2 %fusion.44 = f32[128,2,10,128]{0,3,2,1:T(8,128)S(1)} fusion(f32[128,10,2,640]{3,2,1,0:T(2,128)} %param.8, f32[10,2,128,640]{3,2,1,0:T(8,128)} %param.7, pred[10,2,640]{2,1,0:T(4,128)(4,1)S(1)} %broadcast_compare_fusion), kind=kOutput, calls=%fused_computation.76 | convolution fusion | flops 2518220800 | bytes 14430720 | tf_op jit(solution)/shard_map/jspq,sprq->jpsr/dot_general | solution.py:151
  20.3 33.7 %all_to_all.36 = f32[128,2,10,128]{3,1,2,0:T(2,128)S(1)} all-to-all(f32[128,2,10,128]{3,1,2,0:T(2,128)S(1)} %copy.35), channel_id=1, replica_groups=mesh['lat'=32,'wave'=4] {'lat','wave'}, dimensions={0} | all-to-all | bytes 2621440 | tf_op jit(solution)/shard_map/all_to_all | solution.py:155
  55.2 52.4 %all-gather.2.cloned.1.call-done = f32[4,2,1280,128]{3,2,1,0:T(8,128)} async-done(((f32[1,2,1280,128]{3,2,1,0:T(8,128)}), f32[4,2,1280,128]{3,2,1,0:T(8,128)}) %all-gather.2.cloned.1.call-update) | async-done | bytes 5242896 | tf_op jit(solution)/shard_map/all_gather | solution.py:133
  107.6 270.4 %while.16 = (s32[]{:T(128)}, f32[4,2,1280,128]{3,2,1,0:T(8,128)}, s32[]{:T(128)}, s32[1280]{0:T(1024)S(1)}, s32[4]{0:T(128)S(1)}, /*index=5*/f32[4,2,1280,128]{3...) while((s32[]{:T(128)}, f32[4,2,1280,128]{3,2,1,0:T(8,128)}, s32[]{:T(128)}, ...), condition=%wide.region_1.2_spmd, body=%wide.region_0.1_spmd.sunk | while | flops 11095751680 | bytes 121168528 | solution.py:139
  130.3 8.6 %fusion.60 = (f32[128,1280]{1,0:T(8,128)S(1)}, f32[128,1280]{1,0:T(8,128)S(1)}) fusion(f32[]{:T(128)S(6)} %div.12, s32[]{:T(128)S(6)} %select_n.105, s32[1280]{0:T(1024)S(1)} %get-tuple-element.247, pred[]{:T(512)S(6)} %lt.117), kind=kLoop, calls=%fused_computation.31.clone.1 | loop fusion | flops 1638400 | bytes 1315849 | tf_op jit(solution)/shard_map/while/body/eval_jaxpr/cos | solution.py:72
  139.0 7.0 %multiply_subtract_fusion.2 = (f32[11,128,1280]{2,1,0:T(8,128)}, f32[11,128,1280]{2,1,0:T(8,128)}) fusion(f32[128,1280]{1,0:T(8,128)S(1)} %get-tuple-element.204, f32[11,1280]{1,0:T(8,128)S(1)} %get-tuple-element.205, f32[128,1280]{1,0:T(8,128)S(1)} %get-tuple-element.206, f32[11,1280]{1,0:T(8,128)S(1)} %get-tuple-element.207), kind=kLoop, calls=%fused_computation.4.clone.1 | loop fusion | flops 10813440 | bytes 15841280 | tf_op jit(solution)/shard_map/while/body/eval_jaxpr/while/body/eval_jaxpr/sub | solution.py:82
  145.9 1.5 dynamic-slice_bitcast_fusion.3
  147.5 2.1 slice_multiply_fusion.8
  150.1 18.5 %fusion.62 = f32[1408,128]{0,1:T(8,128)} fusion(f32[1408,1280]{1,0:T(8,128)} %bitcast.40, f32[1408,1280]{1,0:T(8,128)S(1)} %bitcast.38, f32[1280,64]{1,0:T(8,128)} %get-tuple-element.212, f32[1280,64]{1,0:T(8,128)} %get-tuple-element.213, f32[1280,64]{1,0:T(8,128)} %get-tuple-element.214, f32[1280,64]{1,0:T(8,128)} %get-tuple-element.215), kind=kOutput, calls=%fused_computation.2.clone.1 | convolution fusion | flops 5541068800 | bytes 16449536 | tf_op jit(solution)/shard_map/while/body/eval_jaxpr/while/body/eval_jaxpr/dot_general | solution.py:90
  176.8 9.6 %fusion.65 = f32[2560,128]{0,1:T(8,128)} fusion(f32[1408,1280]{1,0:T(8,128)S(1)} %bitcast.43, f32[1408,1280]{1,0:T(8,128)S(1)} %bitcast.39, f32[1408,128]{0,1:T(8,128)S(1)} %multiply_dynamic-update-slice_fusion.17, pred[1408]{0:T(1024)(128)(4,1)S(1)} %add_compare_fusion.2), kind=kOutput, calls=%fused_computation.1.clone.1 | convolution fusion | flops 5540265984 | bytes 16450944 | tf_op jit(solution)/shard_map/while/body/eval_jaxpr/while/body/eval_jaxpr/dot_general | solution.py:104
  193.2 8.6 %fusion.60 = (f32[128,1280]{1,0:T(8,128)S(1)}, f32[128,1280]{1,0:T(8,128)S(1)}) fusion(f32[]{:T(128)S(6)} %div.12, s32[]{:T(128)S(6)} %select_n.105, s32[1280]{0:T(1024)S(1)} %get-tuple-element.247, pred[]{:T(512)S(6)} %lt.117), kind=kLoop, calls=%fused_computation.31.clone.1 | loop fusion | flops 1638400 | bytes 1315849 | tf_op jit(solution)/shard_map/while/body/eval_jaxpr/cos | solution.py:72
  201.8 7.0 %multiply_subtract_fusion.2 = (f32[11,128,1280]{2,1,0:T(8,128)}, f32[11,128,1280]{2,1,0:T(8,128)}) fusion(f32[128,1280]{1,0:T(8,128)S(1)} %get-tuple-element.204, f32[11,1280]{1,0:T(8,128)S(1)} %get-tuple-element.205, f32[128,1280]{1,0:T(8,128)S(1)} %get-tuple-element.206, f32[11,1280]{1,0:T(8,128)S(1)} %get-tuple-element.207), kind=kLoop, calls=%fused_computation.4.clone.1 | loop fusion | flops 10813440 | bytes 15841280 | tf_op jit(solution)/shard_map/while/body/eval_jaxpr/while/body/eval_jaxpr/sub | solution.py:82
  208.7 1.5 dynamic-slice_bitcast_fusion.3
  210.3 2.1 slice_multiply_fusion.8
  212.9 18.5 %fusion.62 = f32[1408,128]{0,1:T(8,128)} fusion(f32[1408,1280]{1,0:T(8,128)} %bitcast.40, f32[1408,1280]{1,0:T(8,128)S(1)} %bitcast.38, f32[1280,64]{1,0:T(8,128)} %get-tuple-element.212, f32[1280,64]{1,0:T(8,128)} %get-tuple-element.213, f32[1280,64]{1,0:T(8,128)} %get-tuple-element.214, f32[1280,64]{1,0:T(8,128)} %get-tuple-element.215), kind=kOutput, calls=%fused_computation.2.clone.1 | convolution fusion | flops 5541068800 | bytes 16449536 | tf_op jit(solution)/shard_map/while/body/eval_jaxpr/while/body/eval_jaxpr/dot_general | solution.py:90
  239.7 9.6 %fusion.65 = f32[2560,128]{0,1:T(8,128)} fusion(f32[1408,1280]{1,0:T(8,128)S(1)} %bitcast.43, f32[1408,1280]{1,0:T(8,128)S(1)} %bitcast.39, f32[1408,128]{0,1:T(8,128)S(1)} %multiply_dynamic-update-slice_fusion.17, pred[1408]{0:T(1024)(128)(4,1)S(1)} %add_compare_fusion.2), kind=kOutput, calls=%fused_computation.1.clone.1 | convolution fusion | flops 5540265984 | bytes 16450944 | tf_op jit(solution)/shard_map/while/body/eval_jaxpr/while/body/eval_jaxpr/dot_general | solution.py:104
  256.0 8.6 %fusion.60 = (f32[128,1280]{1,0:T(8,128)S(1)}, f32[128,1280]{1,0:T(8,128)S(1)}) fusion(f32[]{:T(128)S(6)} %div.12, s32[]{:T(128)S(6)} %select_n.105, s32[1280]{0:T(1024)S(1)} %get-tuple-element.247, pred[]{:T(512)S(6)} %lt.117), kind=kLoop, calls=%fused_computation.31.clone.1 | loop fusion | flops 1638400 | bytes 1315849 | tf_op jit(solution)/shard_map/while/body/eval_jaxpr/cos | solution.py:72
  264.6 7.0 %multiply_subtract_fusion.2 = (f32[11,128,1280]{2,1,0:T(8,128)}, f32[11,128,1280]{2,1,0:T(8,128)}) fusion(f32[128,1280]{1,0:T(8,128)S(1)} %get-tuple-element.204, f32[11,1280]{1,0:T(8,128)S(1)} %get-tuple-element.205, f32[128,1280]{1,0:T(8,128)S(1)} %get-tuple-element.206, f32[11,1280]{1,0:T(8,128)S(1)} %get-tuple-element.207), kind=kLoop, calls=%fused_computation.4.clone.1 | loop fusion | flops 10813440 | bytes 15841280 | tf_op jit(solution)/shard_map/while/body/eval_jaxpr/while/body/eval_jaxpr/sub | solution.py:82
  271.6 1.5 dynamic-slice_bitcast_fusion.3
  273.1 2.1 slice_multiply_fusion.8
  275.8 18.5 %fusion.62 = f32[1408,128]{0,1:T(8,128)} fusion(f32[1408,1280]{1,0:T(8,128)} %bitcast.40, f32[1408,1280]{1,0:T(8,128)S(1)} %bitcast.38, f32[1280,64]{1,0:T(8,128)} %get-tuple-element.212, f32[1280,64]{1,0:T(8,128)} %get-tuple-element.213, f32[1280,64]{1,0:T(8,128)} %get-tuple-element.214, f32[1280,64]{1,0:T(8,128)} %get-tuple-element.215), kind=kOutput, calls=%fused_computation.2.clone.1 | convolution fusion | flops 5541068800 | bytes 16449536 | tf_op jit(solution)/shard_map/while/body/eval_jaxpr/while/body/eval_jaxpr/dot_general | solution.py:90
  302.5 9.6 %fusion.65 = f32[2560,128]{0,1:T(8,128)} fusion(f32[1408,1280]{1,0:T(8,128)S(1)} %bitcast.43, f32[1408,1280]{1,0:T(8,128)S(1)} %bitcast.39, f32[1408,128]{0,1:T(8,128)S(1)} %multiply_dynamic-update-slice_fusion.17, pred[1408]{0:T(1024)(128)(4,1)S(1)} %add_compare_fusion.2), kind=kOutput, calls=%fused_computation.1.clone.1 | convolution fusion | flops 5540265984 | bytes 16450944 | tf_op jit(solution)/shard_map/while/body/eval_jaxpr/while/body/eval_jaxpr/dot_general | solution.py:104
  318.8 8.6 %fusion.60 = (f32[128,1280]{1,0:T(8,128)S(1)}, f32[128,1280]{1,0:T(8,128)S(1)}) fusion(f32[]{:T(128)S(6)} %div.12, s32[]{:T(128)S(6)} %select_n.105, s32[1280]{0:T(1024)S(1)} %get-tuple-element.247, pred[]{:T(512)S(6)} %lt.117), kind=kLoop, calls=%fused_computation.31.clone.1 | loop fusion | flops 1638400 | bytes 1315849 | tf_op jit(solution)/shard_map/while/body/eval_jaxpr/cos | solution.py:72
  327.4 7.0 %multiply_subtract_fusion.2 = (f32[11,128,1280]{2,1,0:T(8,128)}, f32[11,128,1280]{2,1,0:T(8,128)}) fusion(f32[128,1280]{1,0:T(8,128)S(1)} %get-tuple-element.204, f32[11,1280]{1,0:T(8,128)S(1)} %get-tuple-element.205, f32[128,1280]{1,0:T(8,128)S(1)} %get-tuple-element.206, f32[11,1280]{1,0:T(8,128)S(1)} %get-tuple-element.207), kind=kLoop, calls=%fused_computation.4.clone.1 | loop fusion | flops 10813440 | bytes 15841280 | tf_op jit(solution)/shard_map/while/body/eval_jaxpr/while/body/eval_jaxpr/sub | solution.py:82
  334.4 1.5 dynamic-slice_bitcast_fusion.3
  335.9 2.1 slice_multiply_fusion.8
  338.6 18.5 %fusion.62 = f32[1408,128]{0,1:T(8,128)} fusion(f32[1408,1280]{1,0:T(8,128)} %bitcast.40, f32[1408,1280]{1,0:T(8,128)S(1)} %bitcast.38, f32[1280,64]{1,0:T(8,128)} %get-tuple-element.212, f32[1280,64]{1,0:T(8,128)} %get-tuple-element.213, f32[1280,64]{1,0:T(8,128)} %get-tuple-element.214, f32[1280,64]{1,0:T(8,128)} %get-tuple-element.215), kind=kOutput, calls=%fused_computation.2.clone.1 | convolution fusion | flops 5541068800 | bytes 16449536 | tf_op jit(solution)/shard_map/while/body/eval_jaxpr/while/body/eval_jaxpr/dot_general | solution.py:90
  365.3 9.6 %fusion.65 = f32[2560,128]{0,1:T(8,128)} fusion(f32[1408,1280]{1,0:T(8,128)S(1)} %bitcast.43, f32[1408,1280]{1,0:T(8,128)S(1)} %bitcast.39, f32[1408,128]{0,1:T(8,128)S(1)} %multiply_dynamic-update-slice_fusion.17, pred[1408]{0:T(1024)(128)(4,1)S(1)} %add_compare_fusion.2), kind=kOutput, calls=%fused_computation.1.clone.1 | convolution fusion | flops 5540265984 | bytes 16450944 | tf_op jit(solution)/shard_map/while/body/eval_jaxpr/while/body/eval_jaxpr/dot_general | solution.py:104
  378.1 56.0 %reduce-scatter.2.cloned.1.call-done = f32[1,2,1280,128]{3,2,1,0:T(8,128)} async-done(((f32[4,2,1280,128]{3,2,1,0:T(8,128)}), f32[1,2,1280,128]{3,2,1,0:T(8,128)}) %reduce-scatter.2.cloned.1.call-update) | async-done | bytes 1310736 | tf_op jit(solution)/shard_map/reduce_scatter | solution.py:140
  434.1 5.2 %copy.38 = f32[1,2,1280,128]{3,1,0,2:T(2,128)S(1)} copy(f32[1,2,1280,128]{3,2,1,0:T(8,128)} %reduce-scatter.2.cloned.1.call-done) | data formatting | bytes 2621440 | tf_op jit(solution)/shard_map/reduce_scatter | solution.py:140
  439.3 30.2 %all_to_all.37 = f32[1,2,1280,128]{3,1,0,2:T(2,128)S(1)} all-to-all(f32[1,2,1280,128]{3,1,0,2:T(2,128)S(1)} %copy.38), channel_id=1, replica_groups=mesh['lat'=32,'wave'=4] {'lat','wave'}, dimensions={2} | all-to-all | bytes 2621440 | tf_op jit(solution)/shard_map/all_to_all | solution.py:153
  469.8 8.1 %broadcast_select_fusion = f32[10,2,128,640]{3,2,1,0:T(8,128)} fusion(pred[10,2,640]{2,1,0:T(4,128)(4,1)S(1)} %broadcast_compare_fusion, f32[128,10,2,640]{3,2,1,0:T(2,128)S(1)} %bitcast.45, f32[128,1,10,128]{3,0,2,1:T(8,128)S(1)} %get-tuple-element.146, f32[128,1,10,128]{3,0,2,1:T(8,128)S(1)} %get-tuple-element.145, f32[128]{0:T(128)S(1)} %copy-done.2), kind=kOutput, calls=%fused_computation.74 | convolution fusion | flops 2518876160 | bytes 14431232 | tf_op jit(solution)/shard_map/jspq,jpsr->sprq/dot_general | solution.py:167
  (126 shorter events, 58.2 us)
Async XLA Ops:
  6.5 101.1 %all-gather.2.cloned.1.call-start = ((), (), s32[]{:S(2)}) async-start(), calls=%async_computation.3 | async-start | bytes 6553600 | tf_op jit(solution)/shard_map/all_gather | solution.py:133
  18.9 88.7 %copy-start.1 = (s32[1280]{0:T(1024)S(1)}, s32[1280]{0:T(1024)}, u32[]{:S(2)}) copy-start(s32[1280]{0:T(1024)} %param.11) | copy-start | bytes 15364
  19.0 88.7 %copy-start.3 = (s32[4]{0:T(128)S(1)}, s32[4]{0:T(128)}, u32[]{:S(2)}) copy-start(s32[4]{0:T(128)} %param.10) | copy-start | bytes 52
  55.1 379.0 %reduce-scatter.2.cloned.1.call-start = ((), (), s32[]{:S(2)}) async-start(), calls=%async_computation.4 | async-start | bytes 6553600 | tf_op jit(solution)/shard_map/reduce_scatter | solution.py:140
  145.9 4.2 copy-start
  147.5 29.3 %slice-start = ((s8[7208960]{0:T(1024)(128)(4,1)}), s8[4194304]{0:T(1024)(128)(4,1)S(1)}, s32[]{:S(2)}) async-start(s8[7208960]{0:T(1024)(128)(4,1)} %bitcast.41), calls=%async_computation.5 | async-start | bytes 8388608 | tf_op jit(solution)/shard_map/while
  150.1 26.7 %slice-start.1 = ((s8[7208960]{0:T(1024)(128)(4,1)}), s8[3014656]{0:T(1024)(128)(4,1)S(1)}, s32[]{:S(2)}) async-start(s8[7208960]{0:T(1024)(128)(4,1)} %bitcast.41), calls=%async_computation.6 | async-start | bytes 6029312 | tf_op jit(solution)/shard_map/while
  208.7 4.2 copy-start
  210.3 29.3 %slice-start = ((s8[7208960]{0:T(1024)(128)(4,1)}), s8[4194304]{0:T(1024)(128)(4,1)S(1)}, s32[]{:S(2)}) async-start(s8[7208960]{0:T(1024)(128)(4,1)} %bitcast.41), calls=%async_computation.5 | async-start | bytes 8388608 | tf_op jit(solution)/shard_map/while
  212.9 26.7 %slice-start.1 = ((s8[7208960]{0:T(1024)(128)(4,1)}), s8[3014656]{0:T(1024)(128)(4,1)S(1)}, s32[]{:S(2)}) async-start(s8[7208960]{0:T(1024)(128)(4,1)} %bitcast.41), calls=%async_computation.6 | async-start | bytes 6029312 | tf_op jit(solution)/shard_map/while
  271.6 4.2 copy-start
  273.1 29.3 %slice-start = ((s8[7208960]{0:T(1024)(128)(4,1)}), s8[4194304]{0:T(1024)(128)(4,1)S(1)}, s32[]{:S(2)}) async-start(s8[7208960]{0:T(1024)(128)(4,1)} %bitcast.41), calls=%async_computation.5 | async-start | bytes 8388608 | tf_op jit(solution)/shard_map/while
  275.8 26.7 %slice-start.1 = ((s8[7208960]{0:T(1024)(128)(4,1)}), s8[3014656]{0:T(1024)(128)(4,1)S(1)}, s32[]{:S(2)}) async-start(s8[7208960]{0:T(1024)(128)(4,1)} %bitcast.41), calls=%async_computation.6 | async-start | bytes 6029312 | tf_op jit(solution)/shard_map/while
  334.4 4.2 copy-start
  335.9 29.3 %slice-start = ((s8[7208960]{0:T(1024)(128)(4,1)}), s8[4194304]{0:T(1024)(128)(4,1)S(1)}, s32[]{:S(2)}) async-start(s8[7208960]{0:T(1024)(128)(4,1)} %bitcast.41), calls=%async_computation.5 | async-start | bytes 8388608 | tf_op jit(solution)/shard_map/while
  338.6 26.7 %slice-start.1 = ((s8[7208960]{0:T(1024)(128)(4,1)}), s8[3014656]{0:T(1024)(128)(4,1)S(1)}, s32[]{:S(2)}) async-start(s8[7208960]{0:T(1024)(128)(4,1)} %bitcast.41), calls=%async_computation.6 | async-start | bytes 6029312 | tf_op jit(solution)/shard_map/while
  378.0 91.7 %slice-start.2 = ((s8[6553600]{0:T(1024)(128)(4,1)}), s8[2359296]{0:T(1024)(128)(4,1)S(1)}, s32[]{:S(2)}) async-start(s8[6553600]{0:T(1024)(128)(4,1)} %bitcast.44), calls=%async_computation.7 | async-start | bytes 4718592
  378.0 91.7 %copy-start.2 = (f32[128]{0:T(128)S(1)}, f32[128]{0:T(128)}, u32[]{:S(2)}) copy-start(f32[128]{0:T(128)} %param.9) | copy-start | bytes 1540
  439.3 30.5 %slice-start.3 = ((s8[6553600]{0:T(1024)(128)(4,1)}), s8[4194304]{0:T(1024)(128)(4,1)S(1)}, s32[]{:S(2)}) async-start(s8[6553600]{0:T(1024)(128)(4,1)} %bitcast.44), calls=%async_computation.8 | async-start | bytes 8388608
Sparse Core Ops, SparseCore 0:
  55.3 52.3 all-gather.1
  378.2 55.8 reduce-scatter.1
where the time goes:
time: 491 us; the launch traced here: 485 us
  matrix products  132 us (27%)
  other arithmetic  116 us (24%)
  waiting for transfers between devices  108 us (22%)
  blocking collectives  63.9 us (13%)
  loops' own time  26.9 us (5%)
  local copies, waits for them, and re-layouts  24.6 us (5%)
  between operations  13.9 us (3%)
    dot_general x4, matrix products, add_block(): jnp.dot(basis_rows, weighted, precision=HIGHEST_PRECISION, preferred_elem...  74 us
    reduce_scatter x1, waiting for transfers between devices, grid_work(): lax.psum_scatter(partial_sums, 'wave', scatter_dimension=0, tiled=True)  56 us
    all_gather x1, waiting for transfers between devices, grid_work(): group_lines = lax.all_gather(latitude_lines, 'wave', axis=0, tiled=True)  52.4 us
    dot_general x4, matrix products, add_block(): lax.dot_general(basis_rows, terms, (((0,), (0,)), ((), ())), precision=HI...  38.3 us
    cos x4, other arithmetic, pair_cycle(): inner_cosine = jnp.cos(inner_angles)  34.5 us
    all_to_all x1, blocking collectives, body(): lax.all_to_all(fourier, ('lat', 'wave'), split_axis=0, concat_axis=2, til...  33.7 us
    all_to_all x1, blocking collectives, body(): lax.all_to_all(grid_work(lax.all_to_all(fourier, ('lat', 'wave'), split_a...  30.2 us
    sub x4, other arithmetic, add_block(): base_cosine * inner_cosine[None] - base_sine * inner_sine[None]  27.9 us
  transfers between devices with their start and end apart: 2, of which 2 were waited for; matrix products, arithmetic and copies ran while one was open for 0% of the time, Pallas kernels for 0%

commit v1 on v0

v1 whole, which is shorter than its diff:
```python
import functools
import math

import jax
import jax.numpy as jnp
import ml_dtypes
import numpy as np
from jax import lax
from jax.experimental import pallas as pl
from jax.experimental.pallas import tpu as pltpu
from jax.sharding import PartitionSpec as P

WAVES = 1280
SPAN = 256
RADIX = 15
POINTS = RADIX * SPAN
PARTS = WAVES // SPAN
ROUNDS = RADIX // 2 + 1
SLOTS = 10
PAIRS = 128
HALF = 640
DEVICES = 128
OTHERS = DEVICES - 1
MESH = pl.DeviceIdType.MESH
F32 = jnp.float32
BF16 = jnp.bfloat16


def split_host(table):
    high = table.astype(ml_dtypes.bfloat16)
    low = (table - high.astype(np.float64)).astype(ml_dtypes.bfloat16)
    return high, low


@functools.cache
def tables():
    k1 = np.arange(ROUNDS)[:, None, None]
    k2 = np.arange(SPAN)[None, :, None]
    m2 = np.arange(SPAN)[None, None, :]
    angle = 2.0 * np.pi * ((m2 * (k1 + RADIX * k2)) % POINTS) / POINTS
    synthesis = np.concatenate([np.cos(angle), -np.sin(angle)], axis=2)
    analysis = np.ascontiguousarray(np.swapaxes(synthesis, 1, 2))
    turn = 2.0 * np.pi * ((np.arange(ROUNDS)[:, None] * np.arange(PARTS)[None, :]) % RADIX) / RADIX
    turns = np.concatenate([np.cos(turn), np.sin(turn)], axis=1).astype(np.float32).reshape(-1)
    return (*split_host(synthesis), *split_host(analysis), turns)


def halves(value):
    high = value.astype(BF16)
    low = (value - high.astype(F32)).astype(BF16)
    return high, low


def product(high, low, value, transposed=False):
    value_high, value_low = halves(value)
    if transposed:
        numbers = (((1,), (1,)), ((), ()))
        both = jnp.concatenate([value_high, value_low], axis=0)
        width = value.shape[0]
    else:
        numbers = (((1,), (0,)), ((), ()))
        both = jnp.concatenate([value_high, value_low], axis=1)
        width = value.shape[1]
    wide = lax.dot_general(high, both, numbers, preferred_element_type=F32)
    total = wide[:, :width] + wide[:, width:]
    if low is not None:
        total = total + lax.dot_general(low, value_high, numbers, preferred_element_type=F32)
    return total


def peer(step, lat, wave):
    mixed = lax.rem(step * 37, DEVICES)
    z = lax.rem(lat // 8 + mixed // 32, 4)
    y = lax.rem(lax.rem(lat // 2, 4) + lax.rem(mixed // 8, 4), 4)
    core = lax.rem(lax.rem(lat, 2) + lax.rem(mixed // 4, 2), 2)
    x = lax.rem(wave + lax.rem(mixed, 4), 4)
    return z * 8 + y * 2 + core, x


def valid_degrees(number, parity, rows):
    degree = 2 * lax.broadcasted_iota(jnp.int32, (rows, HALF), 1) + parity
    return degree < WAVES - number


def grid_kernel(
    legendre, spectra, assign_scalar, assign_rows, synthesis_high, synthesis_low, analysis_high, analysis_low, turns,
    returned,
    functions, coefficients, forward_high, forward_low, backward_high, backward_low, order, order_back,
    outgoing, incoming, results, waves, sums, load_sem, table_sem, send_sem, receive_sem, own_sem,
):
    lat, wave = lax.axis_index("lat"), lax.axis_index("wave")
    me = lat * 4 + wave
    barrier = pltpu.get_barrier_semaphore()

    def function_copy(slot, parity):
        return pltpu.make_async_copy(legendre.at[:, slot, parity], functions.at[slot, parity], load_sem.at[slot, parity])

    def coefficient_copy(slot, half):
        return pltpu.make_async_copy(
            spectra.at[slot, :, :, :, half], coefficients.at[slot, :, :, half], load_sem.at[slot, 2 + half]
        )

    def start_loads(slot, carry):
        for place in range(2):
            coefficient_copy(slot, place).start()
            function_copy(slot, place).start()
        return carry

    lax.fori_loop(0, SLOTS, start_loads, 0)
    table_copies = [
        pltpu.make_async_copy(source, target, table_sem.at[place])
        for place, (source, target) in enumerate(
            (
                (synthesis_high, forward_high),
                (synthesis_low, forward_low),
                (analysis_high, backward_high),
                (analysis_low, backward_low),
            )
        )
    ]
    for copy in table_copies:
        copy.start()

    def greet(step, carry):
        other_lat, other_wave = peer(step, lat, wave)
        pl.semaphore_signal(barrier, inc=1, device_id=(other_lat, other_wave), device_id_type=MESH)
        return carry

    lax.fori_loop(1, DEVICES, greet, 0)

    lane = lax.broadcasted_iota(jnp.int32, (PAIRS, 128), 1)
    even_block = lax.rem(lane // 32, 2) == 0

    def to_fourier(slot, carry):
        for place in range(2):
            coefficient_copy(slot, place).wait()
            function_copy(slot, place).wait()
        number = assign_scalar[me * SLOTS + slot]
        parts = []
        for parity in range(2):
            values = coefficients[slot, parity].reshape(128, HALF)
            masked = jnp.where(valid_degrees(number, parity, 128), values, 0.0)
            high, low = halves(functions[slot, parity])
            parts.append(product(high, low, masked, transposed=True))
        north, south = parts[0] + parts[1], parts[0] - parts[1]
        rows = pl.ds(slot, PAIRS, stride=SLOTS)
        outgoing[0, rows, :] = jnp.where(even_block, north, pltpu.roll(south, 32, 1))
        outgoing[1, rows, :] = jnp.where(even_block, pltpu.roll(north, 96, 1), south)
        return carry

    lax.fori_loop(0, SLOTS, to_fourier, 0)
    pl.semaphore_wait(barrier, OTHERS)

    def send(source, target, place):
        def one(step, carry):
            other_lat, other_wave = peer(step, lat, wave)
            other = other_lat * 4 + other_wave
            pltpu.make_async_remote_copy(
                source.at[pl.ds(other * SLOTS, SLOTS)],
                target.at[pl.ds(me * SLOTS, SLOTS)],
                send_sem.at[place],
                receive_sem.at[place],
                device_id=(other_lat, other_wave),
                device_id_type=MESH,
            ).start()
            return carry

        lax.fori_loop(1, DEVICES, one, 0)
        mine = pl.ds(me * SLOTS, SLOTS)
        pltpu.make_async_copy(source.at[mine], target.at[mine], own_sem.at[place]).start()

    def settle(source, target, place, sem):
        rows = pl.ds(0, OTHERS * SLOTS)
        pltpu.make_async_copy(source.at[rows], target.at[rows], sem.at[place]).wait()

    def own(source, target, place):
        mine = pl.ds(me * SLOTS, SLOTS)
        pltpu.make_async_copy(source.at[mine], target.at[mine], own_sem.at[place]).wait()

    for half in range(2):
        send(outgoing.at[half], incoming.at[half], half)

    column_of = jnp.transpose(assign_rows[...].astype(F32))

    def build_order(block, carry):
        rows = pl.ds(pl.multiple_of(block * 128, 128), 128)
        number = block * 128 + lax.broadcasted_iota(jnp.int32, (128, 128), 0)
        for place in range(WAVES // 128):
            held = assign_rows[pl.ds(place, 1), :]
            order[rows, pl.ds(place * 128, 128)] = jnp.where(number == held, 1.0, 0.0).astype(BF16)
        return carry

    lax.fori_loop(0, WAVES // 128, build_order, 0)
    for block in range(WAVES // 128):
        held = jnp.broadcast_to(column_of[:, block : block + 1], (128, 128))
        for place in range(WAVES // 128):
            number = (place * 128 + lax.broadcasted_iota(jnp.int32, (128, 128), 1)).astype(F32)
            order_back[pl.ds(block * 128, 128), pl.ds(place * 128, 128)] = jnp.where(held == number, 1.0, 0.0).astype(BF16)

    for copy in table_copies:
        copy.wait()

    span_lane = lax.broadcasted_iota(jnp.int32, (SPAN, 128), 1)
    left = span_lane < 64
    sign = jnp.where(left, 1.0, -1.0)
    field = lax.rem(span_lane // 8, 4)
    first_row = lax.broadcasted_iota(jnp.int32, (SPAN, 128), 0) == 0

    def cross(value):
        return pltpu.roll(value, 64, 1) + sign * value

    for half in range(2):
        settle(outgoing.at[half], incoming.at[half], half, receive_sem)
        own(outgoing.at[half], incoming.at[half], half)
        received = incoming[half]
        received_both = jnp.concatenate(halves(received), axis=1)

        def to_order(part, carry):
            rows = pl.ds(pl.multiple_of(part * SPAN, SPAN), SPAN)
            wide = jnp.dot(order[rows, :], received_both, preferred_element_type=F32)
            value = wide[:, :128] + wide[:, 128:]
            waves[part] = jnp.where(jnp.logical_and(first_row, part == 0), 0.5 * value, value)
            return carry

        lax.fori_loop(0, PARTS, to_order, 0)
        sums[...] = jnp.zeros_like(sums)

        def turn_round(k1, carry):
            cosines = [turns[k1 * 2 * PARTS + part] for part in range(PARTS)]
            sines = [turns[k1 * 2 * PARTS + PARTS + part] for part in range(PARTS)]
            c_sum = waves[0]
            s_sum = sines[1] * waves[1]
            for part in range(1, PARTS):
                c_sum = c_sum + cosines[part] * waves[part]
                if part > 1:
                    s_sum = s_sum + sines[part] * waves[part]
            operand = jnp.concatenate([jnp.where(left, c_sum, -s_sum), jnp.where(left, s_sum, c_sum)], axis=0)
            points = cross(product(forward_high[k1], forward_low[k1], operand))
            other = jnp.where(
                field == 0,
                pltpu.roll(points, 112, 1),
                jnp.where(field == 3, pltpu.roll(points, 16, 1), pltpu.roll(points, 120, 1)),
            )
            doubled = jnp.logical_and(k1 == 0, jnp.logical_not(left))
            terms = cross(jnp.where(doubled, 0.0, points * other))
            found = product(backward_high[k1], backward_low[k1], terms)
            even, odd = found[:SPAN], found[SPAN:]
            c_part = jnp.where(left, even, odd)
            s_part = jnp.where(left, odd, -even)
            sums[0] += c_part
            for part in range(1, PARTS):
                sums[part] += cosines[part] * c_part + sines[part] * s_part
            return carry

        lax.fori_loop(0, ROUNDS, turn_round, 0)
        found_both = jnp.concatenate(halves(sums[...].reshape(WAVES, 128)), axis=1)

        def to_slots(part, carry):
            rows = pl.ds(pl.multiple_of(part * SPAN, SPAN), SPAN)
            wide = jnp.dot(order_back[rows, :], found_both, preferred_element_type=F32)
            results[half, rows, :] = wide[:, :128] + wide[:, 128:]
            return carry

        lax.fori_loop(0, PARTS, to_slots, 0)
        send(results.at[half], returned.at[half], 2 + half)

    for half in range(2):
        settle(outgoing.at[half], incoming.at[half], half, send_sem)
    for half in range(2):
        settle(results.at[half], returned.at[half], 2 + half, receive_sem)
        own(results.at[half], returned.at[half], 2 + half)
        settle(results.at[half], returned.at[half], 2 + half, send_sem)


def harmonic_kernel(own_numbers, legendre, returned, weights, out, functions, load_sem):
    slot = pl.program_id(0)

    def function_copy(place, parity):
        return pltpu.make_async_copy(legendre.at[:, place, parity], functions.at[place, parity], load_sem.at[place, parity])

    @pl.when(slot == 0)
    def _():
        for place in range(SLOTS):
            for parity in range(2):
                function_copy(place, parity).start()

    rows = pl.ds(slot, PAIRS, stride=SLOTS)
    first, second = returned[0, rows, :], returned[1, rows, :]
    even_block = lax.rem(lax.broadcasted_iota(jnp.int32, (PAIRS, 128), 1) // 32, 2) == 0
    first_other, second_other = pltpu.roll(first, 96, 1), pltpu.roll(second, 32, 1)
    scale = weights[...] * (4.0 / POINTS)
    for parity in range(2):
        if parity == 0:
            folded = jnp.where(even_block, first + first_other, second_other + second)
        else:
            folded = jnp.where(even_block, first - first_other, second_other - second)
        high, low = halves(jnp.transpose(folded) * scale)
        function_copy(slot, parity).wait()
        function_high, function_low = halves(functions[slot, parity])
        total = jnp.dot(
            jnp.concatenate([high, low], axis=1),
            jnp.concatenate([function_high, function_high], axis=0),
            preferred_element_type=F32,
        ) + jnp.dot(high, function_low, preferred_element_type=F32)
        total = jnp.where(valid_degrees(own_numbers[slot], parity, 128), total, 0.0)
        for part in range(2):
            for half in range(2):
                for field in range(4):
                    source = ((part * 2 + half) * 4 + field) * 8
                    target = ((part * 4 + field) * 2 + half) * 8
                    out[0, parity, target : target + 8, :] = total[source : source + 8]


def body(spectra, legendre, weights, counts, assign):
    del counts
    *tables_of, turns = tables()
    any_space = pl.BlockSpec(memory_space=pl.ANY)
    scalar = pl.BlockSpec(memory_space=pltpu.SMEM)
    vector = pl.BlockSpec(memory_space=pltpu.VMEM)
    place = lax.axis_index(("lat", "wave"))
    own_numbers = lax.dynamic_slice_in_dim(assign, place * SLOTS, SLOTS)
    returned = pl.pallas_call(
        grid_kernel,
        out_shape=jax.ShapeDtypeStruct((2, WAVES, 128), F32),
        in_specs=[any_space, any_space, scalar, vector, any_space, any_space, any_space, any_space, scalar],
        out_specs=any_space,
        scratch_shapes=[
            pltpu.VMEM((SLOTS, 2, PAIRS, HALF), F32),
            pltpu.VMEM((SLOTS, 2, 2, 2, 4, 8, HALF), F32),
            pltpu.VMEM((ROUNDS, SPAN, 2 * SPAN), BF16),
            pltpu.VMEM((ROUNDS, SPAN, 2 * SPAN), BF16),
            pltpu.VMEM((ROUNDS, 2 * SPAN, SPAN), BF16),
            pltpu.VMEM((ROUNDS, 2 * SPAN, SPAN), BF16),
            pltpu.VMEM((WAVES, WAVES), BF16),
            pltpu.VMEM((WAVES, WAVES), BF16),
            pltpu.VMEM((2, WAVES, 128), F32),
            pltpu.VMEM((2, WAVES, 128), F32),
            pltpu.VMEM((2, WAVES, 128), F32),
            pltpu.VMEM((PARTS, SPAN, 128), F32),
            pltpu.VMEM((PARTS, SPAN, 128), F32),
            pltpu.SemaphoreType.DMA((SLOTS, 4)),
            pltpu.SemaphoreType.DMA((4,)),
            pltpu.SemaphoreType.DMA((4,)),
            pltpu.SemaphoreType.DMA((4,)),
            pltpu.SemaphoreType.DMA((4,)),
        ],
        compiler_params=pltpu.CompilerParams(collective_id=0, has_side_effects=True, vmem_limit_bytes=56 << 20),
        name="grid_round_trip",
    )(
        legendre,
        spectra.reshape(SLOTS, 2, 2, 4, 2, 8, HALF),
        assign,
        jnp.pad(assign.reshape(WAVES // 128, 128), ((0, 6), (0, 0))),
        *(jnp.asarray(table) for table in tables_of),
        jnp.asarray(turns),
    )
    return pl.pallas_call(
        harmonic_kernel,
        grid=(SLOTS,),
        out_shape=jax.ShapeDtypeStruct((SLOTS, 2, 128, HALF), F32),
        in_specs=[
            scalar,
            any_space,
            pl.BlockSpec((2, WAVES, 128), lambda slot: (0, 0, 0)),
            pl.BlockSpec((1, PAIRS), lambda slot: (0, 0)),
        ],
        out_specs=pl.BlockSpec((1, 2, 128, HALF), lambda slot: (slot, 0, 0, 0)),
        scratch_shapes=[pltpu.VMEM((SLOTS, 2, PAIRS, HALF), F32), pltpu.SemaphoreType.DMA((SLOTS, 2))],
        compiler_params=pltpu.CompilerParams(vmem_limit_bytes=40 << 20),
        name="harmonics",
    )(own_numbers, legendre, returned, weights.reshape(1, PAIRS))


def solution(mesh):
    placed = (
        P(("lat", "wave"), None, None, None),
        P(None, ("lat", "wave"), None, None),
        P(),
        P("lat"),
        P(),
    )
    return jax.shard_map(
        body,
        mesh=mesh,
        in_specs=placed,
        out_specs=P(("lat", "wave"), None, None, None),
        check_vma=False,
    )
```

time: 491 us -> 85.8 us (0.17); the launches traced: 485 us -> 85.6 us
  matrix products: 132 us -> 0 us
  other arithmetic: 116 us -> 0 us
  waiting for transfers between devices: 108 us -> 0 us
  Pallas kernels: 0 us -> 82.2 us
  blocking collectives: 63.9 us -> 0 us
  loops' own time: 26.9 us -> 0 us
  local copies, waits for them, and re-layouts: 24.6 us -> 3.39 us
  between operations: 13.9 us -> 0.04 us
    dot_general x10 -> x0, matrix products: 132 us -> none  [the longest x4 74 us: add_block(): jnp.dot(basis_rows, weighted, precision=HIGHEST_PRECISION, preferred_elem...]
    pallas_call x0 -> x2, Pallas kernels: none -> 82.2 us  [the longest x1 68.4 us: body(): pl.pallas_call(grid_kernel, out_shape=jax.ShapeDtypeStruct((2, WAVES, 128...]
    all_to_all x2 -> x0, blocking collectives: 63.9 us -> none  [the longest x1 33.7 us: body(): lax.all_to_all(fourier, ('lat', 'wave'), split_axis=0, concat_axis=2, til...]
    reduce_scatter x1 -> x0, waiting for transfers between devices: 56 us -> none  [grid_work(): lax.psum_scatter(partial_sums, 'wave', scatter_dimension=0, tiled=True)]
    all_gather x1 -> x0, waiting for transfers between devices: 52.4 us -> none  [grid_work(): group_lines = lax.all_gather(latitude_lines, 'wave', axis=0, tiled=True)]
    cos x8 -> x0, other arithmetic: 39.3 us -> none  [the longest x4 34.5 us: pair_cycle(): inner_cosine = jnp.cos(inner_angles)]
    sub x5 -> x0, other arithmetic: 28.7 us -> none  [the longest x4 27.9 us: add_block(): base_cosine * inner_cosine[None] - base_sine * inner_sine[None]]
    another operation x1 -> x0, loops' own time: 26.9 us -> none  [grid_work(): partial_sums = lax.map(per_pair, (group_lines, counts))]
  transfers between devices with their start and end apart: 2 -> 0, of which waited for: 2 -> 0; matrix products, arithmetic and copies ran while one was open for 0% -> 0% of each run, Pallas kernels for 0% -> 0%
where the time goes in v1:
time: 85.8 us; the launch traced here: 85.6 us
  Pallas kernels  82.2 us (96%)
  local copies, waits for them, and re-layouts  3.39 us (4%)
    pallas_call x1, Pallas kernels, body(): pl.pallas_call(grid_kernel, out_shape=jax.ShapeDtypeStruct((2, WAVES, 128...  68.4 us
    pallas_call x1, Pallas kernels, body(): pl.pallas_call(harmonic_kernel, grid=(SLOTS,), out_shape=jax.ShapeDtypeSt...  13.8 us

profile of v1, /device:TPU:1, one launch (start us, length us, event | category | flops | bytes accessed | tf_op | source)
XLA Modules:
  0.0 85.6 jit_solution(15533945119688594925)
XLA Ops:
  0.0 0.8 dynamic_slice.3.own_numbers
  0.8 1.3 %pad.4.assign_rows = s32[16,128]{1,0:T(8,128)} pad(s32[10,128]{1,0:T(8,128)} %bitcast.5, s32[]{:T(128)} %constant.25.clone.1), padding=0_6x0_0 | pad | bytes 13316 | tf_op jit(solution)/shard_map/jit(_pad)/pad | solution.py:353
  2.1 0.0 copy-start
  2.1 0.0 copy-start.2
  2.1 68.4 %grid_round_trip.1.returned = f32[2,1280,128]{2,1,0:T(8,128)} custom-call(f32[128,10,2,640]{3,2,1,0:T(2,128)} %legendre.3, f32[10,2,2,4,2,8,640]{6,5,4,3,2,1,0:T(8,128)} %bitcast.4, s32[1280]{0:T(1024)} %assign_scalar.1, s32[16,128]{1,0:T(8,128)} %pad.4.assign_rows, bf16[8,256,512]{2,1,0:T(8,128)(2,1)} %constant.27.clone.synthesis_high, ...), custom_call_target="tpu_custom_call" | custom-call | tf_op jit(solution)/shard_map/grid_round_trip/pallas_call | solution.py:322
  70.5 0.0 copy-done
  70.5 0.0 copy-done.2
  70.5 0.0 copy-start.1
  70.5 1.3 %copy-done.1 = f32[2,1280,128]{2,1,0:T(8,128)S(1)} copy-done((f32[2,1280,128]{2,1,0:T(8,128)S(1)}, f32[2,1280,128]{2,1,0:T(8,128)}, u32[]{:S(2)}) %copy-start.1) | copy-done | bytes 1310744
  71.8 13.8 %harmonics.1 = f32[10,2,128,640]{3,2,1,0:T(8,128)} custom-call(s32[10]{0:T(128)S(1)} %dynamic_slice.3.own_numbers, f32[128,10,2,640]{3,2,1,0:T(2,128)S(1)} %copy-done, f32[2,1280,128]{2,1,0:T(8,128)S(1)} %copy-done.1, f32[1,128]{1,0:T(1,128)S(1)} %bitcast.3), custom_call_target="tpu_custom_call" | custom-call | tf_op jit(solution)/shard_map/harmonics/pallas_call | solution.py:357
Async XLA Ops:
  2.1 68.4 %copy-start = (f32[128,10,2,640]{3,2,1,0:T(2,128)S(1)}, f32[128,10,2,640]{3,2,1,0:T(2,128)}, u32[]{:S(2)}) copy-start(f32[128,10,2,640]{3,2,1,0:T(2,128)} %legendre.3) | copy-start | bytes 19660804
  2.1 68.4 %copy-start.2 = (f32[128]{0:T(128)S(1)}, f32[128]{0:T(128)}, u32[]{:S(2)}) copy-start(f32[128]{0:T(128)} %param.12) | copy-start | bytes 1540
  70.5 1.3 %copy-start.1 = (f32[2,1280,128]{2,1,0:T(8,128)S(1)}, f32[2,1280,128]{2,1,0:T(8,128)}, u32[]{:S(2)}) copy-start(f32[2,1280,128]{2,1,0:T(8,128)} %grid_round_trip.1.returned) | copy-start | bytes 3932164

commit v2 on v1

v2 whole, which is shorter than its diff:
```python
import functools
import math

import jax
import jax.numpy as jnp
import ml_dtypes
import numpy as np
from jax import lax
from jax.experimental import pallas as pl
from jax.experimental.pallas import tpu as pltpu
from jax.sharding import PartitionSpec as P

WAVES = 1280
SPAN = 256
RADIX = 15
POINTS = RADIX * SPAN
PARTS = WAVES // SPAN
ROUNDS = RADIX // 2 + 1
SLOTS = 10
PAIRS = 128
HALF = 640
DEVICES = 128
OTHERS = DEVICES - 1
MESH = pl.DeviceIdType.MESH
F32 = jnp.float32
BF16 = jnp.bfloat16


def stacked(table):
    high = table.astype(ml_dtypes.bfloat16)
    low = (table - high.astype(np.float64)).astype(ml_dtypes.bfloat16)
    return np.concatenate([high, low], axis=1)


def turn(k1, part):
    angle = 2.0 * math.pi * ((k1 * part) % RADIX) / RADIX
    return math.cos(angle), math.sin(angle)


@functools.cache
def tables():
    k1 = np.arange(ROUNDS)[:, None, None]
    k2 = np.arange(SPAN)[None, :, None]
    m2 = np.arange(SPAN)[None, None, :]
    angle = 2.0 * np.pi * ((m2 * (k1 + RADIX * k2)) % POINTS) / POINTS
    synthesis = np.concatenate([np.cos(angle), -np.sin(angle)], axis=2)
    analysis = np.ascontiguousarray(np.swapaxes(synthesis, 1, 2))
    return stacked(synthesis), stacked(analysis)


def halves(value):
    high = value.astype(BF16)
    low = (value - high.astype(F32)).astype(BF16)
    return high, low


def row_product(high, low, value):
    value_high, value_low = halves(value)
    numbers = (((1,), (1,)), ((), ()))
    both = jnp.concatenate([value_high, value_low], axis=0)
    width = value.shape[0]
    wide = lax.dot_general(high, both, numbers, preferred_element_type=F32)
    total = wide[:, :width] + wide[:, width:]
    return total + lax.dot_general(low, value_high, numbers, preferred_element_type=F32)


def table_product(table, value):
    wide = jnp.dot(table, jnp.concatenate(halves(value), axis=1), preferred_element_type=F32)
    rows, width = wide.shape[0] // 2, value.shape[1]
    return wide[:rows, :width] + (wide[:rows, width:] + wide[rows:, :width])


def peer(step, lat, wave):
    mixed = lax.rem(step * 37, DEVICES)
    z = lax.rem(lat // 8 + mixed // 32, 4)
    y = lax.rem(lax.rem(lat // 2, 4) + lax.rem(mixed // 8, 4), 4)
    core = lax.rem(lax.rem(lat, 2) + lax.rem(mixed // 4, 2), 2)
    x = lax.rem(wave + lax.rem(mixed, 4), 4)
    return z * 8 + y * 2 + core, x


def valid_degrees(number, parity, rows):
    degree = 2 * lax.broadcasted_iota(jnp.int32, (rows, HALF), 1) + parity
    return degree < WAVES - number


def grid_kernel(
    legendre, spectra, assign_scalar, assign, synthesis_table, analysis_table,
    returned, function_high, function_low,
    functions, coefficients, synthesis, analysis, assign_rows, order,
    outgoing, incoming, results, waves, sums, load_sem, table_sem, send_sem, receive_sem, own_sem,
):
    lat, wave = lax.axis_index("lat"), lax.axis_index("wave")
    me = lat * 4 + wave
    barrier = pltpu.get_barrier_semaphore()

    def function_copy(slot, parity):
        return pltpu.make_async_copy(legendre.at[:, slot, parity], functions.at[slot, parity], load_sem.at[slot, parity])

    def coefficient_copy(slot, half):
        return pltpu.make_async_copy(
            spectra.at[slot, :, :, :, half], coefficients.at[slot, :, :, half], load_sem.at[slot, 2 + half]
        )

    def start_loads(slot, carry):
        for place in range(2):
            coefficient_copy(slot, place).start()
            function_copy(slot, place).start()
        return carry

    lax.fori_loop(0, SLOTS, start_loads, 0)
    row_copies = [
        pltpu.make_async_copy(assign.at[pl.ds(row * 128, 128)], assign_rows.at[row], table_sem.at[2 + row])
        for row in range(WAVES // 128)
    ]
    for copy in row_copies:
        copy.start()

    def greet(step, carry):
        other_lat, other_wave = peer(step, lat, wave)
        pl.semaphore_signal(barrier, inc=1, device_id=(other_lat, other_wave), device_id_type=MESH)
        return carry

    lax.fori_loop(1, DEVICES, greet, 0)

    lane = lax.broadcasted_iota(jnp.int32, (PAIRS, 128), 1)
    even_block = lax.rem(lane // 32, 2) == 0

    def to_fourier(slot, carry):
        for place in range(2):
            coefficient_copy(slot, place).wait()
            function_copy(slot, place).wait()
        number = assign_scalar[me * SLOTS + slot]
        parts = []
        for parity in range(2):
            values = coefficients[slot, parity].reshape(128, HALF)
            masked = jnp.where(valid_degrees(number, parity, 128), values, 0.0)
            high, low = halves(functions[slot, parity])
            function_high[slot, parity] = high
            function_low[slot, parity] = low
            parts.append(row_product(high, low, masked))
        north, south = parts[0] + parts[1], parts[0] - parts[1]
        rows = pl.ds(slot, PAIRS, stride=SLOTS)
        outgoing[0, rows, :] = jnp.where(even_block, north, pltpu.roll(south, 32, 1))
        outgoing[1, rows, :] = jnp.where(even_block, pltpu.roll(north, 96, 1), south)
        return carry

    lax.fori_loop(0, SLOTS, to_fourier, 0)
    pl.semaphore_wait(barrier, OTHERS)

    def send(source, target, place, prepare=None):
        def one(step, carry):
            other_lat, other_wave = peer(step, lat, wave)
            other = other_lat * 4 + other_wave
            if prepare is not None:
                prepare(other)
            pltpu.make_async_remote_copy(
                source.at[pl.ds(other * SLOTS, SLOTS)],
                target.at[pl.ds(me * SLOTS, SLOTS)],
                send_sem.at[place],
                receive_sem.at[place],
                device_id=(other_lat, other_wave),
                device_id_type=MESH,
            ).start()
            return carry

        lax.fori_loop(1, DEVICES, one, 0)
        if prepare is not None:
            prepare(me)
        mine = pl.ds(me * SLOTS, SLOTS)
        pltpu.make_async_copy(source.at[mine], target.at[mine], own_sem.at[place]).start()

    def settle(source, target, place, sem):
        rows = pl.ds(0, OTHERS * SLOTS)
        pltpu.make_async_copy(source.at[rows], target.at[rows], sem.at[place]).wait()

    def own(source, target, place):
        mine = pl.ds(me * SLOTS, SLOTS)
        pltpu.make_async_copy(source.at[mine], target.at[mine], own_sem.at[place]).wait()

    for half in range(2):
        send(outgoing.at[half], incoming.at[half], half)

    table_copies = [
        pltpu.make_async_copy(synthesis_table, synthesis, table_sem.at[0]),
        pltpu.make_async_copy(analysis_table, analysis, table_sem.at[1]),
    ]
    for copy in table_copies:
        copy.start()
    for copy in row_copies:
        copy.wait()

    def build_order(block, carry):
        rows = pl.ds(pl.multiple_of(block * 128, 128), 128)
        number = block * 128 + lax.broadcasted_iota(jnp.int32, (128, 128), 0)
        for place in range(WAVES // 128):
            held = assign_rows[pl.ds(place, 1), :]
            order[rows, pl.ds(place * 128, 128)] = jnp.where(number == held, 1.0, 0.0).astype(BF16)
        return carry

    lax.fori_loop(0, WAVES // 128, build_order, 0)
    for copy in table_copies:
        copy.wait()

    span_lane = lax.broadcasted_iota(jnp.int32, (SPAN, 128), 1)
    left = span_lane < 64
    sign = jnp.where(left, 1.0, -1.0)
    field = lax.rem(span_lane // 8, 4)
    first_row = lax.broadcasted_iota(jnp.int32, (SPAN, 128), 0) == 0

    def cross(value):
        return pltpu.roll(value, 64, 1) + sign * value

    for half in range(2):
        settle(outgoing.at[half], incoming.at[half], half, receive_sem)
        own(outgoing.at[half], incoming.at[half], half)
        received = incoming[half]
        received_both = jnp.concatenate(halves(received), axis=1)

        for part in range(PARTS):
            wide = jnp.dot(order[pl.ds(part * SPAN, SPAN), :], received_both, preferred_element_type=F32)
            value = wide[:, :128] + wide[:, 128:]
            waves[part] = jnp.where(first_row, 0.5 * value, value) if part == 0 else value

        for k1 in range(ROUNDS):
            c_sum, s_sum = waves[0], 0.0 * waves[0] if k1 == 0 else 0.0
            for part in range(1, PARTS):
                cosine, sine = turn(k1, part)
                c_sum = c_sum + cosine * waves[part]
                if k1 > 0:
                    s_sum = s_sum + sine * waves[part]
            operand = jnp.concatenate([jnp.where(left, c_sum, -s_sum), jnp.where(left, s_sum, c_sum)], axis=0)
            points = cross(table_product(synthesis[k1], operand))
            other = jnp.where(
                field == 0,
                pltpu.roll(points, 112, 1),
                jnp.where(field == 3, pltpu.roll(points, 16, 1), pltpu.roll(points, 120, 1)),
            )
            terms = points * other
            if k1 == 0:
                terms = jnp.where(left, terms, 0.0)
            found = table_product(analysis[k1], cross(terms))
            even, odd = found[:SPAN], found[SPAN:]
            c_part = jnp.where(left, even, odd)
            s_part = jnp.where(left, odd, -even)
            if k1 == 0:
                for part in range(PARTS):
                    sums[pl.ds(part * SPAN, SPAN), :] = c_part
            else:
                sums[pl.ds(0, SPAN), :] += c_part
                for part in range(1, PARTS):
                    cosine, sine = turn(k1, part)
                    sums[pl.ds(part * SPAN, SPAN), :] += cosine * c_part + sine * s_part

        def to_slots(other):
            for slot in range(SLOTS):
                row = other * SLOTS + slot
                results[half, pl.ds(row, 1), :] = sums[pl.ds(assign_scalar[row], 1), :]

        send(results.at[half], returned.at[half], 2 + half, to_slots)

    for half in range(2):
        settle(outgoing.at[half], incoming.at[half], half, send_sem)
    for half in range(2):
        settle(results.at[half], returned.at[half], 2 + half, receive_sem)
        own(results.at[half], returned.at[half], 2 + half)
        settle(results.at[half], returned.at[half], 2 + half, send_sem)


def harmonic_kernel(assign, function_high, function_low, returned, weights, out, harmonics, store_sem):
    first_number = (lax.axis_index("lat") * 4 + lax.axis_index("wave")) * SLOTS
    even_block = lax.rem(lax.broadcasted_iota(jnp.int32, (PAIRS, 128), 1) // 32, 2) == 0
    scale = weights[...] * (4.0 / POINTS)

    def store_copy(slot):
        return pltpu.make_async_copy(harmonics.at[slot], out.at[slot], store_sem.at[slot])

    def to_harmonics(slot, carry):
        rows = pl.ds(slot, PAIRS, stride=SLOTS)
        first, second = returned[0, rows, :], returned[1, rows, :]
        first_other, second_other = pltpu.roll(first, 96, 1), pltpu.roll(second, 32, 1)
        for parity in range(2):
            if parity == 0:
                folded = jnp.where(even_block, first + first_other, second_other + second)
            else:
                folded = jnp.where(even_block, first - first_other, second_other - second)
            high, low = halves(jnp.transpose(folded) * scale)
            functions = function_high[slot, parity]
            total = jnp.dot(
                jnp.concatenate([high, low], axis=1),
                jnp.concatenate([functions, functions], axis=0),
                preferred_element_type=F32,
            ) + jnp.dot(high, function_low[slot, parity], preferred_element_type=F32)
            total = jnp.where(valid_degrees(assign[first_number + slot], parity, 128), total, 0.0)
            for part in range(2):
                for half in range(2):
                    for field in range(4):
                        source = ((part * 2 + half) * 4 + field) * 8
                        target = ((part * 4 + field) * 2 + half) * 8
                        harmonics[slot, parity, target : target + 8, :] = total[source : source + 8]
        store_copy(slot).start()
        return carry

    lax.fori_loop(0, SLOTS, to_harmonics, 0)
    for slot in range(SLOTS):
        store_copy(slot).wait()


def body(spectra, legendre, weights, counts, assign):
    del counts
    synthesis, analysis = tables()
    any_space = pl.BlockSpec(memory_space=pl.ANY)
    scalar = pl.BlockSpec(memory_space=pltpu.SMEM)
    vector = pl.BlockSpec(memory_space=pltpu.VMEM)
    returned, function_high, function_low = pl.pallas_call(
        grid_kernel,
        out_shape=[
            jax.ShapeDtypeStruct((2, WAVES, 128), F32),
            jax.ShapeDtypeStruct((SLOTS, 2, PAIRS, HALF), BF16),
            jax.ShapeDtypeStruct((SLOTS, 2, PAIRS, HALF), BF16),
        ],
        in_specs=[any_space, any_space, scalar, any_space, any_space, any_space],
        out_specs=[vector, vector, vector],
        scratch_shapes=[
            pltpu.VMEM((SLOTS, 2, PAIRS, HALF), F32),
            pltpu.VMEM((SLOTS, 2, 2, 2, 4, 8, HALF), F32),
            pltpu.VMEM((ROUNDS, 2 * SPAN, 2 * SPAN), BF16),
            pltpu.VMEM((ROUNDS, 4 * SPAN, SPAN), BF16),
            pltpu.VMEM((16, 128), jnp.int32),
            pltpu.VMEM((WAVES, WAVES), BF16),
            pltpu.VMEM((2, WAVES, 128), F32),
            pltpu.VMEM((2, WAVES, 128), F32),
            pltpu.VMEM((2, WAVES, 128), F32),
            pltpu.VMEM((PARTS, SPAN, 128), F32),
            pltpu.VMEM((WAVES, 128), F32),
            pltpu.SemaphoreType.DMA((SLOTS, 4)),
            pltpu.SemaphoreType.DMA((2 + WAVES // 128,)),
            pltpu.SemaphoreType.DMA((4,)),
            pltpu.SemaphoreType.DMA((4,)),
            pltpu.SemaphoreType.DMA((4,)),
        ],
        compiler_params=pltpu.CompilerParams(collective_id=0, has_side_effects=True, vmem_limit_bytes=44 << 20),
        name="grid_round_trip",
    )(legendre, spectra.reshape(SLOTS, 2, 2, 4, 2, 8, HALF), assign, assign, jnp.asarray(synthesis), jnp.asarray(analysis))
    return pl.pallas_call(
        harmonic_kernel,
        out_shape=jax.ShapeDtypeStruct((SLOTS, 2, 128, HALF), F32),
        in_specs=[scalar, vector, vector, vector, vector],
        out_specs=any_space,
        scratch_shapes=[pltpu.VMEM((SLOTS, 2, 128, HALF), F32), pltpu.SemaphoreType.DMA((SLOTS,))],
        compiler_params=pltpu.CompilerParams(vmem_limit_bytes=32 << 20),
        name="harmonics",
    )(assign, function_high, function_low, returned, weights.reshape(1, PAIRS))


def solution(mesh):
    placed = (
        P(("lat", "wave"), None, None, None),
        P(None, ("lat", "wave"), None, None),
        P(),
        P("lat"),
        P(),
    )
    return jax.shard_map(
        body,
        mesh=mesh,
        in_specs=placed,
        out_specs=P(("lat", "wave"), None, None, None),
        check_vma=False,
    )
```

time: 85.8 us -> 65 us (0.76)
  Pallas kernels: 82.2 us -> 64.1 us
  local copies, waits for them, and re-layouts: 3.39 us -> 0.7 us
    pallas_call x2, Pallas kernels: 82.2 us -> 64.1 us  [the longest x1 57.6 us: body(): pl.pallas_call(grid_kernel, out_shape=[jax.ShapeDtypeStruct((2, WAVES, 12...]
    pad x1 -> x0, local copies, waits for them, and re-layouts: 1.3 us -> none  [body(): jnp.pad(assign.reshape(WAVES // 128, 128), ((0, 6), (0, 0)))]
where the time goes in v2:
time: 65 us; the launch traced here: 64.8 us
  Pallas kernels  64.1 us (99%)
  local copies, waits for them, and re-layouts  0.7 us (1%)
    pallas_call x1, Pallas kernels, body(): pl.pallas_call(grid_kernel, out_shape=[jax.ShapeDtypeStruct((2, WAVES, 12...  57.6 us
    pallas_call x1, Pallas kernels, body(): pl.pallas_call(harmonic_kernel, out_shape=jax.ShapeDtypeStruct((SLOTS, 2,...  6.52 us

profile of v2, /device:TPU:1, one launch (start us, length us, event | category | flops | bytes accessed | tf_op | source)
XLA Modules:
  0.0 64.8 jit_solution(16253128253391612749)
XLA Ops:
  0.0 0.0 copy-start
  0.0 0.7 %copy-done = s32[1280]{0:T(1024)S(1)} copy-done((s32[1280]{0:T(1024)S(1)}, s32[1280]{0:T(1024)}, u32[]{:S(2)}) %copy-start) | copy-done | bytes 5144
  0.7 0.0 copy-start.1
  0.7 57.6 %grid_round_trip.1 = (f32[2,1280,128]{2,1,0:T(8,128)S(1)}, bf16[10,2,128,640]{3,2,1,0:T(8,128)(2,1)S(1)}, bf16[10,2,128,640]{3,2,1,0:T(8,128)(2,1)S(1)}) custom-call(f32[128,10,2,640]{3,2,1,0:T(2,128)} %legendre.1, f32[10,2,2,4,2,8,640]{6,5,4,3,2,1,0:T(8,128)} %bitcast.3, s32[1280]{0:T(1024)S(1)} %copy-done, s32[1280]{0:T(1024)S(1)} %copy-done, ...), custom_call_target="tpu_custom_call" | custom-call | tf_op jit(solution)/shard_map/grid_round_trip/pallas_call | solution.py:315
  58.3 0.0 copy-done.1
  58.3 6.5 %harmonics.1 = f32[10,2,128,640]{3,2,1,0:T(8,128)} custom-call(s32[1280]{0:T(1024)S(1)} %copy-done, bf16[10,2,128,640]{3,2,1,0:T(8,128)(2,1)S(1)} %get-tuple-element.8.function_high, bf16[10,2,128,640]{3,2,1,0:T(8,128)(2,1)S(1)} %get-tuple-element.9.function_low, f32[2,1280,128]{2,1,0:T(8,128)S(1)} %get-tuple-element.10.returned, f32[1,128]{1,0:T(1,128)S(1)} %bitcast.2), custom_call_target="tpu_custom_call" | custom-call | tf_op jit(solution)/shard_map/harmonics/pallas_call | solution.py:345
Async XLA Ops:
  0.0 0.7 %copy-start = (s32[1280]{0:T(1024)S(1)}, s32[1280]{0:T(1024)}, u32[]{:S(2)}) copy-start(s32[1280]{0:T(1024)} %assign.3) | copy-start | bytes 15364
  0.7 57.6 %copy-start.1 = (f32[128]{0:T(128)S(1)}, f32[128]{0:T(128)}, u32[]{:S(2)}) copy-start(f32[128]{0:T(128)} %param.9) | copy-start | bytes 1540

commit v3 on v2

--- a/solution.py
+++ b/solution.py
@@ -17,6 +17,7 @@
 PARTS = WAVES // SPAN
 ROUNDS = RADIX // 2 + 1
 SLOTS = 10
+EARLY = 5
 PAIRS = 128
 HALF = 640
 DEVICES = 128
@@ -70,13 +71,20 @@
     return wide[:rows, :width] + (wide[:rows, width:] + wide[rows:, :width])
 
 
-def peer(step, lat, wave):
-    mixed = lax.rem(step * 37, DEVICES)
-    z = lax.rem(lat // 8 + mixed // 32, 4)
-    y = lax.rem(lax.rem(lat // 2, 4) + lax.rem(mixed // 8, 4), 4)
-    core = lax.rem(lax.rem(lat, 2) + lax.rem(mixed // 4, 2), 2)
-    x = lax.rem(wave + lax.rem(mixed, 4), 4)
-    return z * 8 + y * 2 + core, x
+def for_others(lat, wave, act):
+    z, y, core = lat // 8, lax.rem(lat // 2, 4), lax.rem(lat, 2)
+    cores = [core, 1 - core]
+    xs = [lax.rem(wave + offset, 4) for offset in range(4)]
+
+    def group(step, carry, places=range(8)):
+        z_step, y_step = z + step // 4, y + lax.rem(step, 4)
+        for place in places:
+            other_z, other_y = lax.rem(z_step + place, 4), lax.rem(y_step + place // 2, 4)
+            act(other_z * 8 + other_y * 2 + cores[place // 4], xs[place % 4])
+        return carry
+
+    group(0, 0, range(1, 8))
+    lax.fori_loop(1, 16, group, 0)
 
 
 def valid_degrees(number, parity, rows):
@@ -85,9 +93,9 @@
 
 
 def grid_kernel(
-    legendre, spectra, assign_scalar, assign, synthesis_table, analysis_table,
+    legendre, spectra, assign, synthesis_table, analysis_table,
     returned, function_high, function_low,
-    functions, coefficients, synthesis, analysis, assign_rows, order,
+    functions, coefficients, synthesis, analysis, assign_scalar, assign_rows, order,
     outgoing, incoming, results, waves, sums, load_sem, table_sem, send_sem, receive_sem, own_sem,
 ):
     lat, wave = lax.axis_index("lat"), lax.axis_index("wave")
@@ -101,6 +109,9 @@
         return pltpu.make_async_copy(
             spectra.at[slot, :, :, :, half], coefficients.at[slot, :, :, half], load_sem.at[slot, 2 + half]
         )
+
+    scalar_copy = pltpu.make_async_copy(assign, assign_scalar, table_sem.at[2 + WAVES // 128])
+    scalar_copy.start()
 
     def start_loads(slot, carry):
         for place in range(2):
@@ -116,12 +127,10 @@
     for copy in row_copies:
         copy.start()
 
-    def greet(step, carry):
-        other_lat, other_wave = peer(step, lat, wave)
+    def greet(other_lat, other_wave):
         pl.semaphore_signal(barrier, inc=1, device_id=(other_lat, other_wave), device_id_type=MESH)
-        return carry
-
-    lax.fori_loop(1, DEVICES, greet, 0)
+
+    for_others(lat, wave, greet)
 
     lane = lax.broadcasted_iota(jnp.int32, (PAIRS, 128), 1)
     even_block = lax.rem(lane // 32, 2) == 0
@@ -145,41 +154,41 @@
         outgoing[1, rows, :] = jnp.where(even_block, pltpu.roll(north, 96, 1), south)
         return carry
 
-    lax.fori_loop(0, SLOTS, to_fourier, 0)
-    pl.semaphore_wait(barrier, OTHERS)
-
-    def send(source, target, place, prepare=None):
-        def one(step, carry):
-            other_lat, other_wave = peer(step, lat, wave)
+    def send(source, target, place, first=0, count=SLOTS, prepare=None):
+        def one(other_lat, other_wave):
             other = other_lat * 4 + other_wave
             if prepare is not None:
                 prepare(other)
             pltpu.make_async_remote_copy(
-                source.at[pl.ds(other * SLOTS, SLOTS)],
-                target.at[pl.ds(me * SLOTS, SLOTS)],
+                source.at[pl.ds(other * SLOTS + first, count)],
+                target.at[pl.ds(me * SLOTS + first, count)],
                 send_sem.at[place],
                 receive_sem.at[place],
                 device_id=(other_lat, other_wave),
                 device_id_type=MESH,
             ).start()
-            return carry
-
-        lax.fori_loop(1, DEVICES, one, 0)
+
+        for_others(lat, wave, one)
         if prepare is not None:
             prepare(me)
-        mine = pl.ds(me * SLOTS, SLOTS)
+        mine = pl.ds(me * SLOTS + first, count)
         pltpu.make_async_copy(source.at[mine], target.at[mine], own_sem.at[place]).start()
 
-    def settle(source, target, place, sem):
-        rows = pl.ds(0, OTHERS * SLOTS)
+    def settle(source, target, place, sem, count=SLOTS):
+        rows = pl.ds(0, OTHERS * count)
         pltpu.make_async_copy(source.at[rows], target.at[rows], sem.at[place]).wait()
 
-    def own(source, target, place):
-        mine = pl.ds(me * SLOTS, SLOTS)
+    def own(source, target, place, first=0, count=SLOTS):
+        mine = pl.ds(me * SLOTS + first, count)
         pltpu.make_async_copy(source.at[mine], target.at[mine], own_sem.at[place]).wait()
 
-    for half in range(2):
-        send(outgoing.at[half], incoming.at[half], half)
+    scalar_copy.wait()
+    lax.fori_loop(0, EARLY, to_fourier, 0)
+    pl.semaphore_wait(barrier, OTHERS)
+    send(outgoing.at[0], incoming.at[0], 4, 0, EARLY)
+    lax.fori_loop(EARLY, SLOTS, to_fourier, 0)
+    send(outgoing.at[0], incoming.at[0], 0, EARLY, SLOTS - EARLY)
+    send(outgoing.at[1], incoming.at[1], 1)
 
     table_copies = [
         pltpu.make_async_copy(synthesis_table, synthesis, table_sem.at[0]),
@@ -212,8 +221,14 @@
         return pltpu.roll(value, 64, 1) + sign * value
 
     for half in range(2):
-        settle(outgoing.at[half], incoming.at[half], half, receive_sem)
-        own(outgoing.at[half], incoming.at[half], half)
+        if half == 0:
+            settle(outgoing.at[0], incoming.at[0], 4, receive_sem, EARLY)
+            own(outgoing.at[0], incoming.at[0], 4, 0, EARLY)
+            settle(outgoing.at[0], incoming.at[0], 0, receive_sem, SLOTS - EARLY)
+            own(outgoing.at[0], incoming.at[0], 0, EARLY, SLOTS - EARLY)
+        else:
+            settle(outgoing.at[1], incoming.at[1], 1, receive_sem)
+            own(outgoing.at[1], incoming.at[1], 1)
         received = incoming[half]
         received_both = jnp.concatenate(halves(received), axis=1)
 
@@ -257,10 +272,11 @@
                 row = other * SLOTS + slot
                 results[half, pl.ds(row, 1), :] = sums[pl.ds(assign_scalar[row], 1), :]
 
-        send(results.at[half], returned.at[half], 2 + half, to_slots)
-
-    for half in range(2):
-        settle(outgoing.at[half], incoming.at[half], half, send_sem)
+        send(results.at[half], returned.at[half], 2 + half, prepare=to_slots)
+
+    settle(outgoing.at[0], incoming.at[0], 4, send_sem, EARLY)
+    settle(outgoing.at[0], incoming.at[0], 0, send_sem, SLOTS - EARLY)
+    settle(outgoing.at[1], incoming.at[1], 1, send_sem)
     for half in range(2):
         settle(results.at[half], returned.at[half], 2 + half, receive_sem)
         own(results.at[half], returned.at[half], 2 + half)
@@ -301,7 +317,7 @@
         store_copy(slot).start()
         return carry
 
-    lax.fori_loop(0, SLOTS, to_harmonics, 0)
+    lax.fori_loop(0, SLOTS, to_harmonics, 0, unroll=True)
     for slot in range(SLOTS):
         store_copy(slot).wait()
 
@@ -319,13 +335,14 @@
             jax.ShapeDtypeStruct((SLOTS, 2, PAIRS, HALF), BF16),
             jax.ShapeDtypeStruct((SLOTS, 2, PAIRS, HALF), BF16),
         ],
-        in_specs=[any_space, any_space, scalar, any_space, any_space, any_space],
+        in_specs=[any_space, any_space, pl.BlockSpec(memory_space=pltpu.HBM), any_space, any_space],
         out_specs=[vector, vector, vector],
         scratch_shapes=[
             pltpu.VMEM((SLOTS, 2, PAIRS, HALF), F32),
             pltpu.VMEM((SLOTS, 2, 2, 2, 4, 8, HALF), F32),
             pltpu.VMEM((ROUNDS, 2 * SPAN, 2 * SPAN), BF16),
             pltpu.VMEM((ROUNDS, 4 * SPAN, SPAN), BF16),
+            pltpu.SMEM((WAVES,), jnp.int32),
             pltpu.VMEM((16, 128), jnp.int32),
             pltpu.VMEM((WAVES, WAVES), BF16),
             pltpu.VMEM((2, WAVES, 128), F32),
@@ -334,14 +351,14 @@
             pltpu.VMEM((PARTS, SPAN, 128), F32),
             pltpu.VMEM((WAVES, 128), F32),
             pltpu.SemaphoreType.DMA((SLOTS, 4)),
-            pltpu.SemaphoreType.DMA((2 + WAVES // 128,)),
-            pltpu.SemaphoreType.DMA((4,)),
-            pltpu.SemaphoreType.DMA((4,)),
-            pltpu.SemaphoreType.DMA((4,)),
+            pltpu.SemaphoreType.DMA((3 + WAVES // 128,)),
+            pltpu.SemaphoreType.DMA((5,)),
+            pltpu.SemaphoreType.DMA((5,)),
+            pltpu.SemaphoreType.DMA((5,)),
         ],
         compiler_params=pltpu.CompilerParams(collective_id=0, has_side_effects=True, vmem_limit_bytes=44 << 20),
         name="grid_round_trip",
-    )(legendre, spectra.reshape(SLOTS, 2, 2, 4, 2, 8, HALF), assign, assign, jnp.asarray(synthesis), jnp.asarray(analysis))
+    )(legendre, spectra.reshape(SLOTS, 2, 2, 4, 2, 8, HALF), assign, jnp.asarray(synthesis), jnp.asarray(analysis))
     return pl.pallas_call(
         harmonic_kernel,
         out_shape=jax.ShapeDtypeStruct((SLOTS, 2, 128, HALF), F32),

time: 65 us -> 52.1 us (0.80)
  Pallas kernels: 64.1 us -> 51.1 us
    pallas_call x1, Pallas kernels: 57.6 us -> 47.2 us  [body(): pl.pallas_call(grid_kernel, out_shape=[jax.ShapeDtypeStruct((2, WAVES, 12...]
    pallas_call x1, Pallas kernels: 6.52 us -> 3.94 us  [body(): pl.pallas_call(harmonic_kernel, out_shape=jax.ShapeDtypeStruct((SLOTS, 2,...]
where the time goes in v3:
time: 52.1 us; the launch traced here: 52 us
  Pallas kernels  51.1 us (98%)
  local copies, waits for them, and re-layouts  0.7 us (1%)
    pallas_call x1, Pallas kernels, body(): pl.pallas_call(grid_kernel, out_shape=[jax.ShapeDtypeStruct((2, WAVES, 12...  47.2 us
    pallas_call x1, Pallas kernels, body(): pl.pallas_call(harmonic_kernel, out_shape=jax.ShapeDtypeStruct((SLOTS, 2,...  3.94 us

profile of v3, /device:TPU:1, one launch (start us, length us, event | category | flops | bytes accessed | tf_op | source)
XLA Modules:
  0.0 52.0 jit_solution(1513917733173455263)
XLA Ops:
  0.0 0.0 copy-start
  0.0 0.7 %copy-done = s32[1280]{0:T(1024)S(1)} copy-done((s32[1280]{0:T(1024)S(1)}, s32[1280]{0:T(1024)}, u32[]{:S(2)}) %copy-start) | copy-done | bytes 5144
  0.7 0.0 copy-start.1
  0.7 47.2 %grid_round_trip.1 = (f32[2,1280,128]{2,1,0:T(8,128)S(1)}, bf16[10,2,128,640]{3,2,1,0:T(8,128)(2,1)S(1)}, bf16[10,2,128,640]{3,2,1,0:T(8,128)(2,1)S(1)}) custom-call(f32[128,10,2,640]{3,2,1,0:T(2,128)} %legendre.1, f32[10,2,2,4,2,8,640]{6,5,4,3,2,1,0:T(8,128)} %bitcast.3, s32[1280]{0:T(1024)S(1)} %copy-done, ...), custom_call_target="tpu_custom_call" | custom-call | tf_op jit(solution)/shard_map/grid_round_trip/pallas_call | solution.py:331
  47.9 0.0 copy-done.1
  47.9 3.9 %harmonics.1 = f32[10,2,128,640]{3,2,1,0:T(8,128)} custom-call(s32[1280]{0:T(1024)S(1)} %copy-done, bf16[10,2,128,640]{3,2,1,0:T(8,128)(2,1)S(1)} %get-tuple-element.8.function_high, bf16[10,2,128,640]{3,2,1,0:T(8,128)(2,1)S(1)} %get-tuple-element.9.function_low, f32[2,1280,128]{2,1,0:T(8,128)S(1)} %get-tuple-element.10.returned, f32[1,128]{1,0:T(1,128)S(1)} %bitcast.2), custom_call_target="tpu_custom_call" | custom-call | tf_op jit(solution)/shard_map/harmonics/pallas_call | solution.py:362
Async XLA Ops:
  0.0 0.7 %copy-start = (s32[1280]{0:T(1024)S(1)}, s32[1280]{0:T(1024)}, u32[]{:S(2)}) copy-start(s32[1280]{0:T(1024)} %assign.3) | copy-start | bytes 15364
  0.7 47.2 %copy-start.1 = (f32[128]{0:T(128)S(1)}, f32[128]{0:T(128)}, u32[]{:S(2)}) copy-start(f32[128]{0:T(128)} %param.9) | copy-start | bytes 1540

commit v4 on v3

--- a/solution.py
+++ b/solution.py
@@ -17,7 +17,7 @@
 PARTS = WAVES // SPAN
 ROUNDS = RADIX // 2 + 1
 SLOTS = 10
-EARLY = 5
+EARLY = 6
 PAIRS = 128
 HALF = 640
 DEVICES = 128
@@ -119,7 +119,12 @@
             function_copy(slot, place).start()
         return carry
 
-    lax.fori_loop(0, SLOTS, start_loads, 0)
+    lax.fori_loop(0, 2, start_loads, 0)
+    def greet(other_lat, other_wave):
+        pl.semaphore_signal(barrier, inc=1, device_id=(other_lat, other_wave), device_id_type=MESH)
+
+    for_others(lat, wave, greet)
+    lax.fori_loop(2, SLOTS, start_loads, 0)
     row_copies = [
         pltpu.make_async_copy(assign.at[pl.ds(row * 128, 128)], assign_rows.at[row], table_sem.at[2 + row])
         for row in range(WAVES // 128)
@@ -127,10 +132,6 @@
     for copy in row_copies:
         copy.start()
 
-    def greet(other_lat, other_wave):
-        pl.semaphore_signal(barrier, inc=1, device_id=(other_lat, other_wave), device_id_type=MESH)
-
-    for_others(lat, wave, greet)
 
     lane = lax.broadcasted_iota(jnp.int32, (PAIRS, 128), 1)
     even_block = lax.rem(lane // 32, 2) == 0
@@ -183,10 +184,10 @@
         pltpu.make_async_copy(source.at[mine], target.at[mine], own_sem.at[place]).wait()
 
     scalar_copy.wait()
-    lax.fori_loop(0, EARLY, to_fourier, 0)
+    lax.fori_loop(0, EARLY, to_fourier, 0, unroll=True)
     pl.semaphore_wait(barrier, OTHERS)
     send(outgoing.at[0], incoming.at[0], 4, 0, EARLY)
-    lax.fori_loop(EARLY, SLOTS, to_fourier, 0)
+    lax.fori_loop(EARLY, SLOTS, to_fourier, 0, unroll=True)
     send(outgoing.at[0], incoming.at[0], 0, EARLY, SLOTS - EARLY)
     send(outgoing.at[1], incoming.at[1], 1)
 

time: 52.1 us -> 51.8 us (level)
  no operation moved by 1% of the time
where the time goes in v4:
time: 51.8 us; the launch traced here: 51.6 us
  Pallas kernels  50.8 us (98%)
  local copies, waits for them, and re-layouts  0.7 us (1%)
    pallas_call x1, Pallas kernels, body(): pl.pallas_call(grid_kernel, out_shape=[jax.ShapeDtypeStruct((2, WAVES, 12...  46.8 us
    pallas_call x1, Pallas kernels, body(): pl.pallas_call(harmonic_kernel, out_shape=jax.ShapeDtypeStruct((SLOTS, 2,...  3.95 us

profile of v4, /device:TPU:1, one launch (start us, length us, event | category | flops | bytes accessed | tf_op | source)
XLA Modules:
  0.0 51.6 jit_solution(1656759122476923444)
XLA Ops:
  0.0 0.0 copy-start
  0.0 0.7 %copy-done = s32[1280]{0:T(1024)S(1)} copy-done((s32[1280]{0:T(1024)S(1)}, s32[1280]{0:T(1024)}, u32[]{:S(2)}) %copy-start) | copy-done | bytes 5144
  0.7 0.0 copy-start.1
  0.7 46.8 %grid_round_trip.1 = (f32[2,1280,128]{2,1,0:T(8,128)S(1)}, bf16[10,2,128,640]{3,2,1,0:T(8,128)(2,1)S(1)}, bf16[10,2,128,640]{3,2,1,0:T(8,128)(2,1)S(1)}) custom-call(f32[128,10,2,640]{3,2,1,0:T(2,128)} %legendre.1, f32[10,2,2,4,2,8,640]{6,5,4,3,2,1,0:T(8,128)} %bitcast.3, s32[1280]{0:T(1024)S(1)} %copy-done, ...), custom_call_target="tpu_custom_call" | custom-call | tf_op jit(solution)/shard_map/grid_round_trip/pallas_call | solution.py:332
  47.5 0.0 copy-done.1
  47.5 3.9 %harmonics.1 = f32[10,2,128,640]{3,2,1,0:T(8,128)} custom-call(s32[1280]{0:T(1024)S(1)} %copy-done, bf16[10,2,128,640]{3,2,1,0:T(8,128)(2,1)S(1)} %get-tuple-element.8.function_high, bf16[10,2,128,640]{3,2,1,0:T(8,128)(2,1)S(1)} %get-tuple-element.9.function_low, f32[2,1280,128]{2,1,0:T(8,128)S(1)} %get-tuple-element.10.returned, f32[1,128]{1,0:T(1,128)S(1)} %bitcast.2), custom_call_target="tpu_custom_call" | custom-call | tf_op jit(solution)/shard_map/harmonics/pallas_call | solution.py:363
Async XLA Ops:
  0.0 0.7 %copy-start = (s32[1280]{0:T(1024)S(1)}, s32[1280]{0:T(1024)}, u32[]{:S(2)}) copy-start(s32[1280]{0:T(1024)} %assign.3) | copy-start | bytes 15364
  0.7 46.8 %copy-start.1 = (f32[128]{0:T(128)S(1)}, f32[128]{0:T(128)}, u32[]{:S(2)}) copy-start(f32[128]{0:T(128)} %param.9) | copy-start | bytes 1540

commit v5 on v4

--- a/solution.py
+++ b/solution.py
@@ -71,7 +71,7 @@
     return wide[:rows, :width] + (wide[:rows, width:] + wide[rows:, :width])
 
 
-def for_others(lat, wave, act):
+def for_others(lat, wave, act, unroll=1):
     z, y, core = lat // 8, lax.rem(lat // 2, 4), lax.rem(lat, 2)
     cores = [core, 1 - core]
     xs = [lax.rem(wave + offset, 4) for offset in range(4)]
@@ -84,7 +84,7 @@
         return carry
 
     group(0, 0, range(1, 8))
-    lax.fori_loop(1, 16, group, 0)
+    lax.fori_loop(1, 16, group, 0, unroll=unroll)
 
 
 def valid_degrees(number, parity, rows):
@@ -169,7 +169,7 @@
                 device_id_type=MESH,
             ).start()
 
-        for_others(lat, wave, one)
+        for_others(lat, wave, one, 1 if prepare is None else 3)
         if prepare is not None:
             prepare(me)
         mine = pl.ds(me * SLOTS + first, count)
@@ -233,9 +233,10 @@
         received = incoming[half]
         received_both = jnp.concatenate(halves(received), axis=1)
 
+        wide = jnp.dot(order[...], received_both, preferred_element_type=F32)
         for part in range(PARTS):
-            wide = jnp.dot(order[pl.ds(part * SPAN, SPAN), :], received_both, preferred_element_type=F32)
-            value = wide[:, :128] + wide[:, 128:]
+            block = wide[part * SPAN : (part + 1) * SPAN]
+            value = block[:, :128] + block[:, 128:]
             waves[part] = jnp.where(first_row, 0.5 * value, value) if part == 0 else value
 
         for k1 in range(ROUNDS):

time: 51.8 us -> 56.3 us (1.087)
  Pallas kernels: 50.8 us -> 55.3 us
    pallas_call x1, Pallas kernels: 46.8 us -> 51.3 us  [body(): pl.pallas_call(grid_kernel, out_shape=[jax.ShapeDtypeStruct((2, WAVES, 12...]
where the time goes in v5:
time: 56.3 us; the launch traced here: 56.2 us
  Pallas kernels  55.3 us (98%)
  local copies, waits for them, and re-layouts  0.7 us (1%)
    pallas_call x1, Pallas kernels, body(): pl.pallas_call(grid_kernel, out_shape=[jax.ShapeDtypeStruct((2, WAVES, 12...  51.3 us
    pallas_call x1, Pallas kernels, body(): pl.pallas_call(harmonic_kernel, out_shape=jax.ShapeDtypeStruct((SLOTS, 2,...  3.95 us

profile of v5, /device:TPU:1, one launch (start us, length us, event | category | flops | bytes accessed | tf_op | source)
XLA Modules:
  0.0 56.2 jit_solution(5453301688306383641)
XLA Ops:
  0.0 0.0 copy-start
  0.0 0.7 %copy-done = s32[1280]{0:T(1024)S(1)} copy-done((s32[1280]{0:T(1024)S(1)}, s32[1280]{0:T(1024)}, u32[]{:S(2)}) %copy-start) | copy-done | bytes 5144
  0.7 0.0 copy-start.1
  0.7 51.3 %grid_round_trip.1 = (f32[2,1280,128]{2,1,0:T(8,128)S(1)}, bf16[10,2,128,640]{3,2,1,0:T(8,128)(2,1)S(1)}, bf16[10,2,128,640]{3,2,1,0:T(8,128)(2,1)S(1)}) custom-call(f32[128,10,2,640]{3,2,1,0:T(2,128)} %legendre.1, f32[10,2,2,4,2,8,640]{6,5,4,3,2,1,0:T(8,128)} %bitcast.3, s32[1280]{0:T(1024)S(1)} %copy-done, ...), custom_call_target="tpu_custom_call" | custom-call | tf_op jit(solution)/shard_map/grid_round_trip/pallas_call | solution.py:333
  52.0 0.0 copy-done.1
  52.1 3.9 %harmonics.1 = f32[10,2,128,640]{3,2,1,0:T(8,128)} custom-call(s32[1280]{0:T(1024)S(1)} %copy-done, bf16[10,2,128,640]{3,2,1,0:T(8,128)(2,1)S(1)} %get-tuple-element.8.function_high, bf16[10,2,128,640]{3,2,1,0:T(8,128)(2,1)S(1)} %get-tuple-element.9.function_low, f32[2,1280,128]{2,1,0:T(8,128)S(1)} %get-tuple-element.10.returned, f32[1,128]{1,0:T(1,128)S(1)} %bitcast.2), custom_call_target="tpu_custom_call" | custom-call | tf_op jit(solution)/shard_map/harmonics/pallas_call | solution.py:364
Async XLA Ops:
  0.0 0.7 %copy-start = (s32[1280]{0:T(1024)S(1)}, s32[1280]{0:T(1024)}, u32[]{:S(2)}) copy-start(s32[1280]{0:T(1024)} %assign.3) | copy-start | bytes 15364
  0.7 51.3 %copy-start.1 = (f32[128]{0:T(128)S(1)}, f32[128]{0:T(128)}, u32[]{:S(2)}) copy-start(f32[128]{0:T(128)} %param.9) | copy-start | bytes 1540
